TPU v7x, 32 devices: a whole 2x2x4 slice. The times are simulated.
32 devices in a mesh: range: 16 (over z, y, core), height: 2 (over x).
Axes of the slice: x: 2, y: 2, z: 4, core: 2. Of those that a mesh axis runs over, the one named last changes fastest.
Arguments:
- acoustic: float32 [4, 128, 16, 512], P(None, 'range', 'height'), may hold values from -6 to 6
- mean_wind: float32 [3, 128, 16, 512], P(None, 'range', 'height'), may hold values from -0.72 to 0.72
- ground: int32 [128, 512], P('range'), may hold values from 0 to 4, as said below
- shifts: int32 [2], replicated, may hold values from 1 to 2, as said below
Outputs:
- evolved: float32 [4, 128, 16, 512], P(None, 'range', 'height')
Inputs may be any that keep to these rules, and one draw needn't show every extreme that they name: `ground`: some column has exactly 4 solid cells. `shifts`: some step advances by exactly 2 rows.
All inputs are finite; a program needn't handle non-finite values.
Results may differ from a plain program's by a relative error of at most 0.00002.
Values sent between devices are 32-bit elements; how exact they have to be, the bound alone decides.
A program may use at most 64 MiB of HBM per device.

v0:
```python
import jax
import jax.numpy as jnp
from jax import lax
from jax.sharding import PartitionSpec as P

SMAX = 2


FRAME_SPEED = 1.0
TIME_STEP = 0.4
HALF_STEP = 0.2
SIXTH_STEP = 0.4 / 6.0


def extended(cells, sides, width):
    for axis, dim in sides:
        count = lax.axis_size(axis)
        ends = count - 1
        head = lax.slice_in_dim(cells, 0, width, axis=dim)
        tail = lax.slice_in_dim(cells, cells.shape[dim] - width, cells.shape[dim], axis=dim)
        cells = jnp.concatenate(
            [
                lax.ppermute(tail, axis, [(i, (i + 1) % count) for i in range(ends)]),
                cells,
                lax.ppermute(head, axis, [((i + 1) % count, i) for i in range(ends)]),
            ],
            axis=dim,
        )
    return cells


def shifted(array, axis, by):
    length = lax.axis_size(axis)
    return lax.ppermute(array, axis, [(i, (i + by) % length) for i in range(length)])


def central(blocked, along, extent):

    def window(offset):
        return lax.slice_in_dim(blocked, offset, offset + extent, axis=along)

    return (8.0 * (window(3) - window(1)) - (window(4) - window(0))) / 12.0


def tendency(padded, wind_now):
    range_rows = wind_now.shape[1]
    levels = wind_now.shape[2]
    centre = padded[:, 2 : range_rows + 2, 2 : levels + 2, :]
    slope_range = central(padded[:, :, 2 : levels + 2, :], 1, range_rows)
    slope_height = central(padded[:, 2 : range_rows + 2, :, :], 2, levels)
    slope_cross = central(jnp.pad(centre, ((0, 0), (0, 0), (0, 0), (2, 2))), 3, centre.shape[3])
    carried = (
        (wind_now[0] - FRAME_SPEED) * slope_range
        + wind_now[1] * slope_cross
        + wind_now[2] * slope_height
    )
    pressure = -carried[0] - (slope_range[1] + slope_cross[2] + slope_height[3])
    along_range = -carried[1] - slope_range[0]
    along_cross = -carried[2] - slope_cross[0]
    upward = -carried[3] - slope_height[0]
    return jnp.stack([pressure, along_range, along_cross, upward])


def advance_sections(state, current):
    wind_now = current[:3]
    keep_mask = current[3]

    def slope(field):
        padded = extended(field, (("range", 1), ("height", 2)), 2)
        return tendency(padded, wind_now)

    first_slope = slope(state)
    second_state = (state + HALF_STEP * first_slope) * keep_mask
    second_slope = slope(second_state)
    third_state = (state + HALF_STEP * second_slope) * keep_mask
    third_slope = slope(third_state)
    fourth_state = (state + TIME_STEP * third_slope) * keep_mask
    fourth_slope = slope(fourth_state)
    total = first_slope + 2.0 * second_slope + 2.0 * third_slope + fourth_slope
    return (state + SIXTH_STEP * total) * keep_mask


def on_device(acoustic, mean_wind, ground, shifts):
    range_rows = acoustic.shape[1]
    levels = acoustic.shape[2]
    heights = lax.axis_index("height") * levels + jnp.arange(levels, dtype=jnp.int32)
    fluid = (heights[None, :, None] >= ground[:, None, :]).astype(jnp.float32)
    medium = jnp.concatenate([mean_wind, fluid[None]], axis=0)
    steps_count = shifts.shape[0]
    incoming_all = shifted(medium[:, : SMAX * steps_count], "range", -1)
    widened_all = jnp.concatenate([medium, incoming_all], axis=1)
    offsets = jnp.cumsum(shifts)
    state = acoustic
    for step_index in range(steps_count):
        current = lax.dynamic_slice_in_dim(widened_all, offsets[step_index], range_rows, 1)
        state = advance_sections(state, current)
    return state


def solution(mesh):
    in_specs = (
        P(None, "range", "height", None),
        P(None, "range", "height", None),
        P("range", None),
        P(),
    )
    out_specs = P(None, "range", "height", None)
    return jax.shard_map(
        on_device, mesh=mesh, in_specs=in_specs, out_specs=out_specs, check_vma=False
    )
```

profile of v0, /device:TPU:26, one launch (start us, length us, event | category | flops | bytes accessed | tf_op | source)
XLA Modules:
  0.0 171.3 jit_solution(18156146897464094271)
XLA Ops:
  1.5 2.9 %collective-permute-start = (f32[4,2,8,512]{3,1,2,0:T(2,128)S(1)}, f32[4,2,8,512]{3,1,2,0:T(2,128)S(1)}, u32[]{:S(2)}, u32[]{:S(2)}) collective-permute-start(f32[4,2,8,512]{3,1,2,0:T(2,128)S(1)} %get-tuple-element.139), channel_id=1, source_target_pairs={{2,0},{4,2},{6,4},{8,6},{10,8},{12,10},{14,12},{16,14},{18,16},{20... | collective-permute-start | bytes 393224 | tf_op jit(solution)/shard_map/ppermute | solution.py:25
  4.4 1.9 %collective-permute-start.1 = (f32[4,2,8,512]{3,1,2,0:T(2,128)S(1)}, f32[4,2,8,512]{3,1,2,0:T(2,128)S(1)}, u32[]{:S(2)}, u32[]{:S(2)}) collective-permute-start(f32[4,2,8,512]{3,1,2,0:T(2,128)S(1)} %get-tuple-element.140), channel_id=1, source_target_pairs={{0,2},{2,4},{4,6},{6,8},{8,10},{10,12},{12,14},{14,16},{16,18},{18... | collective-permute-start | bytes 393224 | tf_op jit(solution)/shard_map/ppermute | solution.py:23
  6.4 2.7 %collective-permute-start.2 = (f32[4,4,8,512]{3,2,1,0:T(8,128)S(1)}, f32[4,4,8,512]{3,2,1,0:T(8,128)S(1)}, u32[]{:S(2)}, u32[]{:S(2)}) collective-permute-start(f32[4,4,8,512]{3,2,1,0:T(8,128)S(1)} %pad_maximum_fusion.94), channel_id=1, source_target_pairs={{0,30},{2,0},{4,2},{6,4},{8,6},{10,8},{12,10},{14,12},{16,14},{18,... | collective-permute-start | bytes 786440 | tf_op jit(solution)/shard_map/ppermute | solution.py:34
  13.7 2.5 %collective-permute-start.3 = (f32[4,12,2,512]{3,1,2,0:T(8,128)S(1)}, f32[4,12,2,512]{3,1,2,0:T(8,128)S(1)}, u32[]{:S(2)}, u32[]{:S(2)}) collective-permute-start(f32[4,12,2,512]{3,1,2,0:T(8,128)S(1)} %get-tuple-element.107), channel_id=1, source_target_pairs={{1,0},{3,2},{5,4},{7,6},{9,8},{11,10},{13,12},{15,14},{17,16},{19,... | collective-permute-start | bytes 589832 | tf_op jit(solution)/shard_map/ppermute | solution.py:25
  20.6 4.1 %collective-permute-done.4 = f32[4,12,2,512]{3,1,2,0:T(8,128)S(1)} collective-permute-done((f32[4,12,2,512]{3,1,2,0:T(8,128)S(1)}, f32[4,12,2,512]{3,1,2,0:T(8,128)S(1)}, u32[]{:S(2)}, u32[]{:S(2)}) %collective-permute-start.4) | collective-permute-done | bytes 196640 | tf_op jit(solution)/shard_map/ppermute | solution.py:23
  26.7 3.7 %collective-permute-start.5 = (f32[4,2,8,512]{3,1,2,0:T(2,128)S(1)}, f32[4,2,8,512]{3,1,2,0:T(2,128)S(1)}, u32[]{:S(2)}, u32[]{:S(2)}) collective-permute-start(f32[4,2,8,512]{3,1,2,0:T(2,128)S(1)} %get-tuple-element.135), channel_id=1, source_target_pairs={{2,0},{4,2},{6,4},{8,6},{10,8},{12,10},{14,12},{16,14},{18,16},{20... | collective-permute-start | bytes 393224 | tf_op jit(solution)/shard_map/ppermute | solution.py:25
  30.4 1.9 %collective-permute-start.6 = (f32[4,2,8,512]{3,1,2,0:T(2,128)S(1)}, f32[4,2,8,512]{3,1,2,0:T(2,128)S(1)}, u32[]{:S(2)}, u32[]{:S(2)}) collective-permute-start(f32[4,2,8,512]{3,1,2,0:T(2,128)S(1)} %get-tuple-element.136), channel_id=1, source_target_pairs={{0,2},{2,4},{4,6},{6,8},{8,10},{10,12},{12,14},{14,16},{16,18},{18... | collective-permute-start | bytes 393224 | tf_op jit(solution)/shard_map/ppermute | solution.py:23
  32.9 4.7 %collective-permute-done.6 = f32[4,2,8,512]{3,1,2,0:T(2,128)S(1)} collective-permute-done((f32[4,2,8,512]{3,1,2,0:T(2,128)S(1)}, f32[4,2,8,512]{3,1,2,0:T(2,128)S(1)}, u32[]{:S(2)}, u32[]{:S(2)}) %collective-permute-start.6) | collective-permute-done | bytes 131104 | tf_op jit(solution)/shard_map/ppermute | solution.py:23
  43.2 4.4 %collective-permute-done.8 = f32[4,12,2,512]{3,1,2,0:T(8,128)S(1)} collective-permute-done((f32[4,12,2,512]{3,1,2,0:T(8,128)S(1)}, f32[4,12,2,512]{3,1,2,0:T(8,128)S(1)}, u32[]{:S(2)}, u32[]{:S(2)}) %collective-permute-start.8) | collective-permute-done | bytes 196640 | tf_op jit(solution)/shard_map/ppermute | solution.py:23
  48.6 1.9 %collective-permute-start.9 = (f32[4,2,8,512]{3,1,2,0:T(2,128)S(1)}, f32[4,2,8,512]{3,1,2,0:T(2,128)S(1)}, u32[]{:S(2)}, u32[]{:S(2)}) collective-permute-start(f32[4,2,8,512]{3,1,2,0:T(2,128)S(1)} %get-tuple-element.131), channel_id=1, source_target_pairs={{2,0},{4,2},{6,4},{8,6},{10,8},{12,10},{14,12},{16,14},{18,16},{20... | collective-permute-start | bytes 393224 | tf_op jit(solution)/shard_map/ppermute | solution.py:25
  50.6 2.4 %collective-permute-start.10 = (f32[4,2,8,512]{3,1,2,0:T(2,128)S(1)}, f32[4,2,8,512]{3,1,2,0:T(2,128)S(1)}, u32[]{:S(2)}, u32[]{:S(2)}) collective-permute-start(f32[4,2,8,512]{3,1,2,0:T(2,128)S(1)} %get-tuple-element.132), channel_id=1, source_target_pairs={{0,2},{2,4},{4,6},{6,8},{8,10},{10,12},{12,14},{14,16},{16,18},{18... | collective-permute-start | bytes 393224 | tf_op jit(solution)/shard_map/ppermute | solution.py:23
  53.1 4.7 %collective-permute-done.10 = f32[4,2,8,512]{3,1,2,0:T(2,128)S(1)} collective-permute-done((f32[4,2,8,512]{3,1,2,0:T(2,128)S(1)}, f32[4,2,8,512]{3,1,2,0:T(2,128)S(1)}, u32[]{:S(2)}, u32[]{:S(2)}) %collective-permute-start.10) | collective-permute-done | bytes 131104 | tf_op jit(solution)/shard_map/ppermute | solution.py:23
  63.2 4.4 %collective-permute-done.12 = f32[4,12,2,512]{3,1,2,0:T(8,128)S(1)} collective-permute-done((f32[4,12,2,512]{3,1,2,0:T(8,128)S(1)}, f32[4,12,2,512]{3,1,2,0:T(8,128)S(1)}, u32[]{:S(2)}, u32[]{:S(2)}) %collective-permute-start.12) | collective-permute-done | bytes 196640 | tf_op jit(solution)/shard_map/ppermute | solution.py:23
  68.6 1.9 %collective-permute-start.13 = (f32[4,2,8,512]{3,1,2,0:T(2,128)S(1)}, f32[4,2,8,512]{3,1,2,0:T(2,128)S(1)}, u32[]{:S(2)}, u32[]{:S(2)}) collective-permute-start(f32[4,2,8,512]{3,1,2,0:T(2,128)S(1)} %get-tuple-element.127), channel_id=1, source_target_pairs={{2,0},{4,2},{6,4},{8,6},{10,8},{12,10},{14,12},{16,14},{18,16},{20... | collective-permute-start | bytes 393224 | tf_op jit(solution)/shard_map/ppermute | solution.py:25
  70.6 2.4 %collective-permute-start.14 = (f32[4,2,8,512]{3,1,2,0:T(2,128)S(1)}, f32[4,2,8,512]{3,1,2,0:T(2,128)S(1)}, u32[]{:S(2)}, u32[]{:S(2)}) collective-permute-start(f32[4,2,8,512]{3,1,2,0:T(2,128)S(1)} %get-tuple-element.128), channel_id=1, source_target_pairs={{0,2},{2,4},{4,6},{6,8},{8,10},{10,12},{12,14},{14,16},{16,18},{18... | collective-permute-start | bytes 393224 | tf_op jit(solution)/shard_map/ppermute | solution.py:23
  73.1 4.7 %collective-permute-done.14 = f32[4,2,8,512]{3,1,2,0:T(2,128)S(1)} collective-permute-done((f32[4,2,8,512]{3,1,2,0:T(2,128)S(1)}, f32[4,2,8,512]{3,1,2,0:T(2,128)S(1)}, u32[]{:S(2)}, u32[]{:S(2)}) %collective-permute-start.14) | collective-permute-done | bytes 131104 | tf_op jit(solution)/shard_map/ppermute | solution.py:23
  83.2 4.4 %collective-permute-done.16 = f32[4,12,2,512]{3,1,2,0:T(8,128)S(1)} collective-permute-done((f32[4,12,2,512]{3,1,2,0:T(8,128)S(1)}, f32[4,12,2,512]{3,1,2,0:T(8,128)S(1)}, u32[]{:S(2)}, u32[]{:S(2)}) %collective-permute-start.16) | collective-permute-done | bytes 196640 | tf_op jit(solution)/shard_map/ppermute | solution.py:23
  88.8 1.9 %collective-permute-start.17 = (f32[4,2,8,512]{3,1,2,0:T(2,128)S(1)}, f32[4,2,8,512]{3,1,2,0:T(2,128)S(1)}, u32[]{:S(2)}, u32[]{:S(2)}) collective-permute-start(f32[4,2,8,512]{3,1,2,0:T(2,128)S(1)} %get-tuple-element.123), channel_id=1, source_target_pairs={{2,0},{4,2},{6,4},{8,6},{10,8},{12,10},{14,12},{16,14},{18,16},{20... | collective-permute-start | bytes 393224 | tf_op jit(solution)/shard_map/ppermute | solution.py:25
  90.8 2.4 %collective-permute-start.18 = (f32[4,2,8,512]{3,1,2,0:T(2,128)S(1)}, f32[4,2,8,512]{3,1,2,0:T(2,128)S(1)}, u32[]{:S(2)}, u32[]{:S(2)}) collective-permute-start(f32[4,2,8,512]{3,1,2,0:T(2,128)S(1)} %get-tuple-element.124), channel_id=1, source_target_pairs={{0,2},{2,4},{4,6},{6,8},{8,10},{10,12},{12,14},{14,16},{16,18},{18... | collective-permute-start | bytes 393224 | tf_op jit(solution)/shard_map/ppermute | solution.py:23
  93.3 4.7 %collective-permute-done.18 = f32[4,2,8,512]{3,1,2,0:T(2,128)S(1)} collective-permute-done((f32[4,2,8,512]{3,1,2,0:T(2,128)S(1)}, f32[4,2,8,512]{3,1,2,0:T(2,128)S(1)}, u32[]{:S(2)}, u32[]{:S(2)}) %collective-permute-start.18) | collective-permute-done | bytes 131104 | tf_op jit(solution)/shard_map/ppermute | solution.py:23
  103.4 4.4 %collective-permute-done.20 = f32[4,12,2,512]{3,1,2,0:T(8,128)S(1)} collective-permute-done((f32[4,12,2,512]{3,1,2,0:T(8,128)S(1)}, f32[4,12,2,512]{3,1,2,0:T(8,128)S(1)}, u32[]{:S(2)}, u32[]{:S(2)}) %collective-permute-start.20) | collective-permute-done | bytes 196640 | tf_op jit(solution)/shard_map/ppermute | solution.py:23
  109.1 1.9 %collective-permute-start.21 = (f32[4,2,8,512]{3,1,2,0:T(2,128)S(1)}, f32[4,2,8,512]{3,1,2,0:T(2,128)S(1)}, u32[]{:S(2)}, u32[]{:S(2)}) collective-permute-start(f32[4,2,8,512]{3,1,2,0:T(2,128)S(1)} %get-tuple-element.119), channel_id=1, source_target_pairs={{2,0},{4,2},{6,4},{8,6},{10,8},{12,10},{14,12},{16,14},{18,16},{20... | collective-permute-start | bytes 393224 | tf_op jit(solution)/shard_map/ppermute | solution.py:25
  111.1 2.4 %collective-permute-start.22 = (f32[4,2,8,512]{3,1,2,0:T(2,128)S(1)}, f32[4,2,8,512]{3,1,2,0:T(2,128)S(1)}, u32[]{:S(2)}, u32[]{:S(2)}) collective-permute-start(f32[4,2,8,512]{3,1,2,0:T(2,128)S(1)} %get-tuple-element.120), channel_id=1, source_target_pairs={{0,2},{2,4},{4,6},{6,8},{8,10},{10,12},{12,14},{14,16},{16,18},{18... | collective-permute-start | bytes 393224 | tf_op jit(solution)/shard_map/ppermute | solution.py:23
  113.6 4.7 %collective-permute-done.22 = f32[4,2,8,512]{3,1,2,0:T(2,128)S(1)} collective-permute-done((f32[4,2,8,512]{3,1,2,0:T(2,128)S(1)}, f32[4,2,8,512]{3,1,2,0:T(2,128)S(1)}, u32[]{:S(2)}, u32[]{:S(2)}) %collective-permute-start.22) | collective-permute-done | bytes 131104 | tf_op jit(solution)/shard_map/ppermute | solution.py:23
  123.7 4.4 %collective-permute-done.24 = f32[4,12,2,512]{3,1,2,0:T(8,128)S(1)} collective-permute-done((f32[4,12,2,512]{3,1,2,0:T(8,128)S(1)}, f32[4,12,2,512]{3,1,2,0:T(8,128)S(1)}, u32[]{:S(2)}, u32[]{:S(2)}) %collective-permute-start.24) | collective-permute-done | bytes 196640 | tf_op jit(solution)/shard_map/ppermute | solution.py:23
  129.4 1.9 %collective-permute-start.25 = (f32[4,2,8,512]{3,1,2,0:T(2,128)S(1)}, f32[4,2,8,512]{3,1,2,0:T(2,128)S(1)}, u32[]{:S(2)}, u32[]{:S(2)}) collective-permute-start(f32[4,2,8,512]{3,1,2,0:T(2,128)S(1)} %get-tuple-element.115), channel_id=1, source_target_pairs={{2,0},{4,2},{6,4},{8,6},{10,8},{12,10},{14,12},{16,14},{18,16},{20... | collective-permute-start | bytes 393224 | tf_op jit(solution)/shard_map/ppermute | solution.py:25
  131.4 2.4 %collective-permute-start.26 = (f32[4,2,8,512]{3,1,2,0:T(2,128)S(1)}, f32[4,2,8,512]{3,1,2,0:T(2,128)S(1)}, u32[]{:S(2)}, u32[]{:S(2)}) collective-permute-start(f32[4,2,8,512]{3,1,2,0:T(2,128)S(1)} %get-tuple-element.116), channel_id=1, source_target_pairs={{0,2},{2,4},{4,6},{6,8},{8,10},{10,12},{12,14},{14,16},{16,18},{18... | collective-permute-start | bytes 393224 | tf_op jit(solution)/shard_map/ppermute | solution.py:23
  133.9 4.7 %collective-permute-done.26 = f32[4,2,8,512]{3,1,2,0:T(2,128)S(1)} collective-permute-done((f32[4,2,8,512]{3,1,2,0:T(2,128)S(1)}, f32[4,2,8,512]{3,1,2,0:T(2,128)S(1)}, u32[]{:S(2)}, u32[]{:S(2)}) %collective-permute-start.26) | collective-permute-done | bytes 131104 | tf_op jit(solution)/shard_map/ppermute | solution.py:23
  144.0 4.4 %collective-permute-done.28 = f32[4,12,2,512]{3,1,2,0:T(8,128)S(1)} collective-permute-done((f32[4,12,2,512]{3,1,2,0:T(8,128)S(1)}, f32[4,12,2,512]{3,1,2,0:T(8,128)S(1)}, u32[]{:S(2)}, u32[]{:S(2)}) %collective-permute-start.28) | collective-permute-done | bytes 196640 | tf_op jit(solution)/shard_map/ppermute | solution.py:23
  151.7 2.4 %collective-permute-start.30 = (f32[4,2,8,512]{3,1,2,0:T(2,128)S(1)}, f32[4,2,8,512]{3,1,2,0:T(2,128)S(1)}, u32[]{:S(2)}, u32[]{:S(2)}) collective-permute-start(f32[4,2,8,512]{3,1,2,0:T(2,128)S(1)} %get-tuple-element.112), channel_id=1, source_target_pairs={{0,2},{2,4},{4,6},{6,8},{8,10},{10,12},{12,14},{14,16},{16,18},{18... | collective-permute-start | bytes 393224 | tf_op jit(solution)/shard_map/ppermute | solution.py:23
  154.2 4.7 %collective-permute-done.30 = f32[4,2,8,512]{3,1,2,0:T(2,128)S(1)} collective-permute-done((f32[4,2,8,512]{3,1,2,0:T(2,128)S(1)}, f32[4,2,8,512]{3,1,2,0:T(2,128)S(1)}, u32[]{:S(2)}, u32[]{:S(2)}) %collective-permute-start.30) | collective-permute-done | bytes 131104 | tf_op jit(solution)/shard_map/ppermute | solution.py:23
  164.3 4.4 %collective-permute-done.32 = f32[4,12,2,512]{3,1,2,0:T(8,128)S(1)} collective-permute-done((f32[4,12,2,512]{3,1,2,0:T(8,128)S(1)}, f32[4,12,2,512]{3,1,2,0:T(8,128)S(1)}, u32[]{:S(2)}, u32[]{:S(2)}) %collective-permute-start.32) | collective-permute-done | bytes 196640 | tf_op jit(solution)/shard_map/ppermute | solution.py:23
  (116 shorter events, 59.4 us)
Async XLA Ops:
  1.5 12.1 %collective-permute-start = (f32[4,2,8,512]{3,1,2,0:T(2,128)S(1)}, f32[4,2,8,512]{3,1,2,0:T(2,128)S(1)}, u32[]{:S(2)}, u32[]{:S(2)}) collective-permute-start(f32[4,2,8,512]{3,1,2,0:T(2,128)S(1)} %get-tuple-element.139), channel_id=1, source_target_pairs={{2,0},{4,2},{6,4},{8,6},{10,8},{12,10},{14,12},{16,14},{18,16},{20... | collective-permute-start | bytes 393224 | tf_op jit(solution)/shard_map/ppermute | solution.py:25
  4.4 9.2 %collective-permute-start.1 = (f32[4,2,8,512]{3,1,2,0:T(2,128)S(1)}, f32[4,2,8,512]{3,1,2,0:T(2,128)S(1)}, u32[]{:S(2)}, u32[]{:S(2)}) collective-permute-start(f32[4,2,8,512]{3,1,2,0:T(2,128)S(1)} %get-tuple-element.140), channel_id=1, source_target_pairs={{0,2},{2,4},{4,6},{6,8},{8,10},{10,12},{12,14},{14,16},{16,18},{18... | collective-permute-start | bytes 393224 | tf_op jit(solution)/shard_map/ppermute | solution.py:23
  6.4 11.9 %collective-permute-start.2 = (f32[4,4,8,512]{3,2,1,0:T(8,128)S(1)}, f32[4,4,8,512]{3,2,1,0:T(8,128)S(1)}, u32[]{:S(2)}, u32[]{:S(2)}) collective-permute-start(f32[4,4,8,512]{3,2,1,0:T(8,128)S(1)} %pad_maximum_fusion.94), channel_id=1, source_target_pairs={{0,30},{2,0},{4,2},{6,4},{8,6},{10,8},{12,10},{14,12},{16,14},{18,... | collective-permute-start | bytes 786440 | tf_op jit(solution)/shard_map/ppermute | solution.py:34
  13.7 6.9 %collective-permute-start.3 = (f32[4,12,2,512]{3,1,2,0:T(8,128)S(1)}, f32[4,12,2,512]{3,1,2,0:T(8,128)S(1)}, u32[]{:S(2)}, u32[]{:S(2)}) collective-permute-start(f32[4,12,2,512]{3,1,2,0:T(8,128)S(1)} %get-tuple-element.107), channel_id=1, source_target_pairs={{1,0},{3,2},{5,4},{7,6},{9,8},{11,10},{13,12},{15,14},{17,16},{19,... | collective-permute-start | bytes 589832 | tf_op jit(solution)/shard_map/ppermute | solution.py:25
  16.1 8.6 %collective-permute-start.4 = (f32[4,12,2,512]{3,1,2,0:T(8,128)S(1)}, f32[4,12,2,512]{3,1,2,0:T(8,128)S(1)}, u32[]{:S(2)}, u32[]{:S(2)}) collective-permute-start(f32[4,12,2,512]{3,1,2,0:T(8,128)S(1)} %get-tuple-element.108), channel_id=1, source_target_pairs={{0,1},{2,3},{4,5},{6,7},{8,9},{10,11},{12,13},{14,15},{16,17},{18,... | collective-permute-start | bytes 589832 | tf_op jit(solution)/shard_map/ppermute | solution.py:23
  26.7 6.2 %collective-permute-start.5 = (f32[4,2,8,512]{3,1,2,0:T(2,128)S(1)}, f32[4,2,8,512]{3,1,2,0:T(2,128)S(1)}, u32[]{:S(2)}, u32[]{:S(2)}) collective-permute-start(f32[4,2,8,512]{3,1,2,0:T(2,128)S(1)} %get-tuple-element.135), channel_id=1, source_target_pairs={{2,0},{4,2},{6,4},{8,6},{10,8},{12,10},{14,12},{16,14},{18,16},{20... | collective-permute-start | bytes 393224 | tf_op jit(solution)/shard_map/ppermute | solution.py:25
  30.4 7.2 %collective-permute-start.6 = (f32[4,2,8,512]{3,1,2,0:T(2,128)S(1)}, f32[4,2,8,512]{3,1,2,0:T(2,128)S(1)}, u32[]{:S(2)}, u32[]{:S(2)}) collective-permute-start(f32[4,2,8,512]{3,1,2,0:T(2,128)S(1)} %get-tuple-element.136), channel_id=1, source_target_pairs={{0,2},{2,4},{4,6},{6,8},{8,10},{10,12},{12,14},{14,16},{16,18},{18... | collective-permute-start | bytes 393224 | tf_op jit(solution)/shard_map/ppermute | solution.py:23
  37.7 5.5 %collective-permute-start.7 = (f32[4,12,2,512]{3,1,2,0:T(8,128)S(1)}, f32[4,12,2,512]{3,1,2,0:T(8,128)S(1)}, u32[]{:S(2)}, u32[]{:S(2)}) collective-permute-start(f32[4,12,2,512]{3,1,2,0:T(8,128)S(1)} %get-tuple-element.105), channel_id=1, source_target_pairs={{1,0},{3,2},{5,4},{7,6},{9,8},{11,10},{13,12},{15,14},{17,16},{19,... | collective-permute-start | bytes 589832 | tf_op jit(solution)/shard_map/ppermute | solution.py:25
  39.3 8.3 %collective-permute-start.8 = (f32[4,12,2,512]{3,1,2,0:T(8,128)S(1)}, f32[4,12,2,512]{3,1,2,0:T(8,128)S(1)}, u32[]{:S(2)}, u32[]{:S(2)}) collective-permute-start(f32[4,12,2,512]{3,1,2,0:T(8,128)S(1)} %get-tuple-element.106), channel_id=1, source_target_pairs={{0,1},{2,3},{4,5},{6,7},{8,9},{10,11},{12,13},{14,15},{16,17},{18,... | collective-permute-start | bytes 589832 | tf_op jit(solution)/shard_map/ppermute | solution.py:23
  48.6 4.4 %collective-permute-start.9 = (f32[4,2,8,512]{3,1,2,0:T(2,128)S(1)}, f32[4,2,8,512]{3,1,2,0:T(2,128)S(1)}, u32[]{:S(2)}, u32[]{:S(2)}) collective-permute-start(f32[4,2,8,512]{3,1,2,0:T(2,128)S(1)} %get-tuple-element.131), channel_id=1, source_target_pairs={{2,0},{4,2},{6,4},{8,6},{10,8},{12,10},{14,12},{16,14},{18,16},{20... | collective-permute-start | bytes 393224 | tf_op jit(solution)/shard_map/ppermute | solution.py:25
  50.6 7.2 %collective-permute-start.10 = (f32[4,2,8,512]{3,1,2,0:T(2,128)S(1)}, f32[4,2,8,512]{3,1,2,0:T(2,128)S(1)}, u32[]{:S(2)}, u32[]{:S(2)}) collective-permute-start(f32[4,2,8,512]{3,1,2,0:T(2,128)S(1)} %get-tuple-element.132), channel_id=1, source_target_pairs={{0,2},{2,4},{4,6},{6,8},{8,10},{10,12},{12,14},{14,16},{16,18},{18... | collective-permute-start | bytes 393224 | tf_op jit(solution)/shard_map/ppermute | solution.py:23
  57.8 5.3 %collective-permute-start.11 = (f32[4,12,2,512]{3,1,2,0:T(8,128)S(1)}, f32[4,12,2,512]{3,1,2,0:T(8,128)S(1)}, u32[]{:S(2)}, u32[]{:S(2)}) collective-permute-start(f32[4,12,2,512]{3,1,2,0:T(8,128)S(1)} %get-tuple-element.103), channel_id=1, source_target_pairs={{1,0},{3,2},{5,4},{7,6},{9,8},{11,10},{13,12},{15,14},{17,16},{19,... | collective-permute-start | bytes 589832 | tf_op jit(solution)/shard_map/ppermute | solution.py:25
  59.3 8.3 %collective-permute-start.12 = (f32[4,12,2,512]{3,1,2,0:T(8,128)S(1)}, f32[4,12,2,512]{3,1,2,0:T(8,128)S(1)}, u32[]{:S(2)}, u32[]{:S(2)}) collective-permute-start(f32[4,12,2,512]{3,1,2,0:T(8,128)S(1)} %get-tuple-element.104), channel_id=1, source_target_pairs={{0,1},{2,3},{4,5},{6,7},{8,9},{10,11},{12,13},{14,15},{16,17},{18,... | collective-permute-start | bytes 589832 | tf_op jit(solution)/shard_map/ppermute | solution.py:23
  68.6 4.4 %collective-permute-start.13 = (f32[4,2,8,512]{3,1,2,0:T(2,128)S(1)}, f32[4,2,8,512]{3,1,2,0:T(2,128)S(1)}, u32[]{:S(2)}, u32[]{:S(2)}) collective-permute-start(f32[4,2,8,512]{3,1,2,0:T(2,128)S(1)} %get-tuple-element.127), channel_id=1, source_target_pairs={{2,0},{4,2},{6,4},{8,6},{10,8},{12,10},{14,12},{16,14},{18,16},{20... | collective-permute-start | bytes 393224 | tf_op jit(solution)/shard_map/ppermute | solution.py:25
  70.6 7.2 %collective-permute-start.14 = (f32[4,2,8,512]{3,1,2,0:T(2,128)S(1)}, f32[4,2,8,512]{3,1,2,0:T(2,128)S(1)}, u32[]{:S(2)}, u32[]{:S(2)}) collective-permute-start(f32[4,2,8,512]{3,1,2,0:T(2,128)S(1)} %get-tuple-element.128), channel_id=1, source_target_pairs={{0,2},{2,4},{4,6},{6,8},{8,10},{10,12},{12,14},{14,16},{16,18},{18... | collective-permute-start | bytes 393224 | tf_op jit(solution)/shard_map/ppermute | solution.py:23
  77.9 5.3 %collective-permute-start.15 = (f32[4,12,2,512]{3,1,2,0:T(8,128)S(1)}, f32[4,12,2,512]{3,1,2,0:T(8,128)S(1)}, u32[]{:S(2)}, u32[]{:S(2)}) collective-permute-start(f32[4,12,2,512]{3,1,2,0:T(8,128)S(1)} %get-tuple-element.101), channel_id=1, source_target_pairs={{1,0},{3,2},{5,4},{7,6},{9,8},{11,10},{13,12},{15,14},{17,16},{19,... | collective-permute-start | bytes 589832 | tf_op jit(solution)/shard_map/ppermute | solution.py:25
  79.3 8.3 %collective-permute-start.16 = (f32[4,12,2,512]{3,1,2,0:T(8,128)S(1)}, f32[4,12,2,512]{3,1,2,0:T(8,128)S(1)}, u32[]{:S(2)}, u32[]{:S(2)}) collective-permute-start(f32[4,12,2,512]{3,1,2,0:T(8,128)S(1)} %get-tuple-element.102), channel_id=1, source_target_pairs={{0,1},{2,3},{4,5},{6,7},{8,9},{10,11},{12,13},{14,15},{16,17},{18,... | collective-permute-start | bytes 589832 | tf_op jit(solution)/shard_map/ppermute | solution.py:23
  90.8 7.2 %collective-permute-start.18 = (f32[4,2,8,512]{3,1,2,0:T(2,128)S(1)}, f32[4,2,8,512]{3,1,2,0:T(2,128)S(1)}, u32[]{:S(2)}, u32[]{:S(2)}) collective-permute-start(f32[4,2,8,512]{3,1,2,0:T(2,128)S(1)} %get-tuple-element.124), channel_id=1, source_target_pairs={{0,2},{2,4},{4,6},{6,8},{8,10},{10,12},{12,14},{14,16},{16,18},{18... | collective-permute-start | bytes 393224 | tf_op jit(solution)/shard_map/ppermute | solution.py:23
  98.0 5.3 %collective-permute-start.19 = (f32[4,12,2,512]{3,1,2,0:T(8,128)S(1)}, f32[4,12,2,512]{3,1,2,0:T(8,128)S(1)}, u32[]{:S(2)}, u32[]{:S(2)}) collective-permute-start(f32[4,12,2,512]{3,1,2,0:T(8,128)S(1)} %get-tuple-element.99), channel_id=1, source_target_pairs={{1,0},{3,2},{5,4},{7,6},{9,8},{11,10},{13,12},{15,14},{17,16},{19,... | collective-permute-start | bytes 589832 | tf_op jit(solution)/shard_map/ppermute | solution.py:25
  99.5 8.3 %collective-permute-start.20 = (f32[4,12,2,512]{3,1,2,0:T(8,128)S(1)}, f32[4,12,2,512]{3,1,2,0:T(8,128)S(1)}, u32[]{:S(2)}, u32[]{:S(2)}) collective-permute-start(f32[4,12,2,512]{3,1,2,0:T(8,128)S(1)} %get-tuple-element.100), channel_id=1, source_target_pairs={{0,1},{2,3},{4,5},{6,7},{8,9},{10,11},{12,13},{14,15},{16,17},{18,... | collective-permute-start | bytes 589832 | tf_op jit(solution)/shard_map/ppermute | solution.py:23
  109.1 4.4 %collective-permute-start.21 = (f32[4,2,8,512]{3,1,2,0:T(2,128)S(1)}, f32[4,2,8,512]{3,1,2,0:T(2,128)S(1)}, u32[]{:S(2)}, u32[]{:S(2)}) collective-permute-start(f32[4,2,8,512]{3,1,2,0:T(2,128)S(1)} %get-tuple-element.119), channel_id=1, source_target_pairs={{2,0},{4,2},{6,4},{8,6},{10,8},{12,10},{14,12},{16,14},{18,16},{20... | collective-permute-start | bytes 393224 | tf_op jit(solution)/shard_map/ppermute | solution.py:25
  111.1 7.2 %collective-permute-start.22 = (f32[4,2,8,512]{3,1,2,0:T(2,128)S(1)}, f32[4,2,8,512]{3,1,2,0:T(2,128)S(1)}, u32[]{:S(2)}, u32[]{:S(2)}) collective-permute-start(f32[4,2,8,512]{3,1,2,0:T(2,128)S(1)} %get-tuple-element.120), channel_id=1, source_target_pairs={{0,2},{2,4},{4,6},{6,8},{8,10},{10,12},{12,14},{14,16},{16,18},{18... | collective-permute-start | bytes 393224 | tf_op jit(solution)/shard_map/ppermute | solution.py:23
  118.3 5.3 %collective-permute-start.23 = (f32[4,12,2,512]{3,1,2,0:T(8,128)S(1)}, f32[4,12,2,512]{3,1,2,0:T(8,128)S(1)}, u32[]{:S(2)}, u32[]{:S(2)}) collective-permute-start(f32[4,12,2,512]{3,1,2,0:T(8,128)S(1)} %get-tuple-element.89), channel_id=1, source_target_pairs={{1,0},{3,2},{5,4},{7,6},{9,8},{11,10},{13,12},{15,14},{17,16},{19,... | collective-permute-start | bytes 589832 | tf_op jit(solution)/shard_map/ppermute | solution.py:25
  119.8 8.3 %collective-permute-start.24 = (f32[4,12,2,512]{3,1,2,0:T(8,128)S(1)}, f32[4,12,2,512]{3,1,2,0:T(8,128)S(1)}, u32[]{:S(2)}, u32[]{:S(2)}) collective-permute-start(f32[4,12,2,512]{3,1,2,0:T(8,128)S(1)} %get-tuple-element.90), channel_id=1, source_target_pairs={{0,1},{2,3},{4,5},{6,7},{8,9},{10,11},{12,13},{14,15},{16,17},{18,... | collective-permute-start | bytes 589832 | tf_op jit(solution)/shard_map/ppermute | solution.py:23
  129.4 4.4 %collective-permute-start.25 = (f32[4,2,8,512]{3,1,2,0:T(2,128)S(1)}, f32[4,2,8,512]{3,1,2,0:T(2,128)S(1)}, u32[]{:S(2)}, u32[]{:S(2)}) collective-permute-start(f32[4,2,8,512]{3,1,2,0:T(2,128)S(1)} %get-tuple-element.115), channel_id=1, source_target_pairs={{2,0},{4,2},{6,4},{8,6},{10,8},{12,10},{14,12},{16,14},{18,16},{20... | collective-permute-start | bytes 393224 | tf_op jit(solution)/shard_map/ppermute | solution.py:25
  131.4 7.2 %collective-permute-start.26 = (f32[4,2,8,512]{3,1,2,0:T(2,128)S(1)}, f32[4,2,8,512]{3,1,2,0:T(2,128)S(1)}, u32[]{:S(2)}, u32[]{:S(2)}) collective-permute-start(f32[4,2,8,512]{3,1,2,0:T(2,128)S(1)} %get-tuple-element.116), channel_id=1, source_target_pairs={{0,2},{2,4},{4,6},{6,8},{8,10},{10,12},{12,14},{14,16},{16,18},{18... | collective-permute-start | bytes 393224 | tf_op jit(solution)/shard_map/ppermute | solution.py:23
  138.6 5.3 %collective-permute-start.27 = (f32[4,12,2,512]{3,1,2,0:T(8,128)S(1)}, f32[4,12,2,512]{3,1,2,0:T(8,128)S(1)}, u32[]{:S(2)}, u32[]{:S(2)}) collective-permute-start(f32[4,12,2,512]{3,1,2,0:T(8,128)S(1)} %get-tuple-element.87), channel_id=1, source_target_pairs={{1,0},{3,2},{5,4},{7,6},{9,8},{11,10},{13,12},{15,14},{17,16},{19,... | collective-permute-start | bytes 589832 | tf_op jit(solution)/shard_map/ppermute | solution.py:25
  140.1 8.3 %collective-permute-start.28 = (f32[4,12,2,512]{3,1,2,0:T(8,128)S(1)}, f32[4,12,2,512]{3,1,2,0:T(8,128)S(1)}, u32[]{:S(2)}, u32[]{:S(2)}) collective-permute-start(f32[4,12,2,512]{3,1,2,0:T(8,128)S(1)} %get-tuple-element.88), channel_id=1, source_target_pairs={{0,1},{2,3},{4,5},{6,7},{8,9},{10,11},{12,13},{14,15},{16,17},{18,... | collective-permute-start | bytes 589832 | tf_op jit(solution)/shard_map/ppermute | solution.py:23
  149.7 4.4 %collective-permute-start.29 = (f32[4,2,8,512]{3,1,2,0:T(2,128)S(1)}, f32[4,2,8,512]{3,1,2,0:T(2,128)S(1)}, u32[]{:S(2)}, u32[]{:S(2)}) collective-permute-start(f32[4,2,8,512]{3,1,2,0:T(2,128)S(1)} %get-tuple-element.111), channel_id=1, source_target_pairs={{2,0},{4,2},{6,4},{8,6},{10,8},{12,10},{14,12},{16,14},{18,16},{20... | collective-permute-start | bytes 393224 | tf_op jit(solution)/shard_map/ppermute | solution.py:25
  151.7 7.2 %collective-permute-start.30 = (f32[4,2,8,512]{3,1,2,0:T(2,128)S(1)}, f32[4,2,8,512]{3,1,2,0:T(2,128)S(1)}, u32[]{:S(2)}, u32[]{:S(2)}) collective-permute-start(f32[4,2,8,512]{3,1,2,0:T(2,128)S(1)} %get-tuple-element.112), channel_id=1, source_target_pairs={{0,2},{2,4},{4,6},{6,8},{8,10},{10,12},{12,14},{14,16},{16,18},{18... | collective-permute-start | bytes 393224 | tf_op jit(solution)/shard_map/ppermute | solution.py:23
  158.9 5.3 %collective-permute-start.31 = (f32[4,12,2,512]{3,1,2,0:T(8,128)S(1)}, f32[4,12,2,512]{3,1,2,0:T(8,128)S(1)}, u32[]{:S(2)}, u32[]{:S(2)}) collective-permute-start(f32[4,12,2,512]{3,1,2,0:T(8,128)S(1)} %get-tuple-element.85), channel_id=1, source_target_pairs={{1,0},{3,2},{5,4},{7,6},{9,8},{11,10},{13,12},{15,14},{17,16},{19,... | collective-permute-start | bytes 589832 | tf_op jit(solution)/shard_map/ppermute | solution.py:25
  160.4 8.3 %collective-permute-start.32 = (f32[4,12,2,512]{3,1,2,0:T(8,128)S(1)}, f32[4,12,2,512]{3,1,2,0:T(8,128)S(1)}, u32[]{:S(2)}, u32[]{:S(2)}) collective-permute-start(f32[4,12,2,512]{3,1,2,0:T(8,128)S(1)} %get-tuple-element.86), channel_id=1, source_target_pairs={{0,1},{2,3},{4,5},{6,7},{8,9},{10,11},{12,13},{14,15},{16,17},{18,... | collective-permute-start | bytes 589832 | tf_op jit(solution)/shard_map/ppermute | solution.py:23
  (5 other events, 18.2 us)
where the time goes:
time: 172 us; the launch traced here: 171 us
  waiting for transfers between devices  81.1 us (47%)
  starting transfers between devices  62.5 us (36%)
  other arithmetic  18 us (10%)
  local copies, waits for them, and re-layouts  5.32 us (3%)
  between operations  4.44 us (3%)
    ppermute x16, waiting for transfers between devices, extended(): lax.ppermute(tail, axis, [(i, (i + 1) % count) for i in range(ends)])  67.8 us
    ppermute x16, starting transfers between devices, extended(): lax.ppermute(head, axis, [((i + 1) % count, i) for i in range(ends)])  31 us
    ppermute x16, starting transfers between devices, extended(): lax.ppermute(tail, axis, [(i, (i + 1) % count) for i in range(ends)])  28.8 us
    ppermute x16, waiting for transfers between devices, extended(): lax.ppermute(head, axis, [((i + 1) % count, i) for i in range(ends)])  13.3 us
    div x16, other arithmetic, central(): return (8.0 * (window(3) - window(1)) - (window(4) - window(0))) / 12.0  8.03 us
  transfers between devices with their start and end apart: 33, of which 30 were waited for; matrix products, arithmetic and copies ran while one was open for 6% of the time, Pallas kernels for 0%

commit v1 on v0

v1 whole, which is shorter than its diff:
```python
import functools

import jax
import jax.numpy as jnp
from jax import lax
from jax.experimental import pallas as pl
from jax.experimental.pallas import tpu as pltpu
from jax.sharding import PartitionSpec as P

SMAX = 2
MESH = pl.DeviceIdType.MESH
LANES = 128
SUB = 8


def kernel(
    n_range, n_height, steps,
    shifts_ref, a_ref, w_in, g_in, o_ref,
    cur, base, acc, wind, mask, ground, pack, halo, send_sem, recv_sem, wsend, wrecv,
):
    rows, levels, width = a_ref.shape[1], a_ref.shape[2], a_ref.shape[3]
    tiles, blocks = levels // SUB, width // LANES
    extra = SMAX * steps
    me, hi = lax.axis_index("range"), lax.axis_index("height")
    below, above = me - 1, me + 1
    wrap_below = lax.rem(me + n_range - 1, n_range)
    wrap_above = lax.rem(me + 1, n_range)
    has_below, has_above = me > 0, me < n_range - 1
    has_down, has_up = hi > 0, hi < n_height - 1

    sub = lax.broadcasted_iota(jnp.int32, (SUB, LANES), 0)
    lane = lax.broadcasted_iota(jnp.int32, (SUB, LANES), 1)

    barrier = pltpu.get_barrier_semaphore()
    pl.semaphore_signal(barrier, inc=1, device_id={"range": wrap_below}, device_id_type=MESH)
    pl.semaphore_signal(barrier, inc=1, device_id={"range": wrap_above}, device_id_type=MESH)

    @pl.when(has_down)
    def _():
        pl.semaphore_signal(barrier, inc=1, device_id={"height": hi - 1}, device_id_type=MESH)

    @pl.when(has_up)
    def _():
        pl.semaphore_signal(barrier, inc=1, device_id={"height": hi + 1}, device_id_type=MESH)

    def pack_row(slot, field, row, low, high):
        down, up = low[0], None
        for j in range(blocks):
            up_j = pltpu.roll(high[j], (2 * j - (SUB - 2)) % SUB, 0)
            if j == 0:
                up = up_j
                continue
            here = (sub >= 2 * j)
            down = jnp.where(here, pltpu.roll(low[j], 2 * j, 0), down)
            up = jnp.where(here, up_j, up)
        pack[slot, 0, field, row] = down
        pack[slot, 1, field, row] = up

    def load_row(row, carry):
        for f in range(4):
            for t in range(tiles):
                cur[0, f, row + 2, t * SUB:(t + 1) * SUB, :] = a_ref[f, row, t * SUB:(t + 1) * SUB, :]
            low = [a_ref[f, row, 0:SUB, j * LANES:(j + 1) * LANES] for j in range(blocks)]
            high = [a_ref[f, row, levels - SUB:levels, j * LANES:(j + 1) * LANES] for j in range(blocks)]
            pack_row(0, f, row, low, high)
        return carry

    lax.fori_loop(0, rows, load_row, 0)

    nothing = jnp.zeros((SUB, width), jnp.float32)

    @pl.when(jnp.logical_not(has_below))
    def _():
        for s in range(2):
            for f in range(4):
                for r in range(2):
                    for t in range(tiles):
                        cur[s, f, r, t * SUB:(t + 1) * SUB, :] = nothing

    @pl.when(jnp.logical_not(has_above))
    def _():
        for s in range(2):
            for f in range(4):
                for r in range(2):
                    for t in range(tiles):
                        cur[s, f, rows + 2 + r, t * SUB:(t + 1) * SUB, :] = nothing

    small = jnp.zeros((SUB, LANES), jnp.float32)

    @pl.when(jnp.logical_not(has_down))
    def _():
        for s in range(2):
            for f in range(4):
                for r in range(rows):
                    halo[s, 0, f, r] = small

    @pl.when(jnp.logical_not(has_up))
    def _():
        for s in range(2):
            for f in range(4):
                for r in range(rows):
                    halo[s, 1, f, r] = small

    pl.semaphore_wait(barrier, 2 + has_down.astype(jnp.int32) + has_up.astype(jnp.int32))

    def to_below(slot):
        return pltpu.make_async_remote_copy(
            src_ref=cur.at[slot, :, pl.ds(2, 2)], dst_ref=cur.at[slot, :, pl.ds(rows + 2, 2)],
            send_sem=send_sem.at[slot, 0], recv_sem=recv_sem.at[slot, 0],
            device_id={"range": below}, device_id_type=MESH)

    def to_above(slot):
        return pltpu.make_async_remote_copy(
            src_ref=cur.at[slot, :, pl.ds(rows, 2)], dst_ref=cur.at[slot, :, pl.ds(0, 2)],
            send_sem=send_sem.at[slot, 1], recv_sem=recv_sem.at[slot, 1],
            device_id={"range": above}, device_id_type=MESH)

    spans = [(0, 2), (2, rows - 4), (rows - 2, 2)]

    def to_down(slot, part):
        first, count = spans[part]
        return pltpu.make_async_remote_copy(
            src_ref=pack.at[slot, 0, :, pl.ds(first, count)], dst_ref=halo.at[slot, 1, :, pl.ds(first, count)],
            send_sem=send_sem.at[slot, 2 + part], recv_sem=recv_sem.at[slot, 2 + part],
            device_id={"height": hi - 1}, device_id_type=MESH)

    def to_up(slot, part):
        first, count = spans[part]
        return pltpu.make_async_remote_copy(
            src_ref=pack.at[slot, 1, :, pl.ds(first, count)], dst_ref=halo.at[slot, 0, :, pl.ds(first, count)],
            send_sem=send_sem.at[slot, 5 + part], recv_sem=recv_sem.at[slot, 5 + part],
            device_id={"height": hi + 1}, device_id_type=MESH)

    def send_height(slot, part):
        pl.when(has_down)(lambda: to_down(slot, part).start())
        pl.when(has_up)(lambda: to_up(slot, part).start())

    def recv_height(slot, part):
        pl.when(has_up)(lambda: to_down(slot, part).wait_recv())
        pl.when(has_down)(lambda: to_up(slot, part).wait_recv())

    def drain(slot):
        def down():
            for part in range(3):
                to_down(slot, part).wait_send()

        def up():
            for part in range(3):
                to_up(slot, part).wait_send()

        pl.when(has_below)(lambda: to_below(slot).wait_send())
        pl.when(has_above)(lambda: to_above(slot).wait_send())
        pl.when(has_down)(down)
        pl.when(has_up)(up)

    def wind_copy(step):
        return pltpu.make_async_remote_copy(
            src_ref=w_in.at[:, pl.ds(SMAX * step, SMAX)], dst_ref=wind.at[:, pl.ds(rows + SMAX * step, SMAX)],
            send_sem=wsend.at[step], recv_sem=wrecv.at[step],
            device_id={"range": wrap_below}, device_id_type=MESH)

    ground_copy = pltpu.make_async_remote_copy(
        src_ref=g_in, dst_ref=ground, send_sem=wsend.at[steps], recv_sem=wrecv.at[steps],
        device_id={"range": wrap_below}, device_id_type=MESH)

    pl.when(has_below)(lambda: to_below(0).start())
    pl.when(has_above)(lambda: to_above(0).start())
    for part in (1, 0, 2):
        send_height(0, part)
    ground_copy.start()
    for step in range(steps):
        wind_copy(step).start()

    def own_wind(row, carry):
        for c in range(3):
            for t in range(tiles):
                wind[c, row, t * SUB:(t + 1) * SUB, :] = w_in[c, row, t * SUB:(t + 1) * SUB, :]
        return carry

    lax.fori_loop(0, rows, own_wind, 0)
    level = lax.broadcasted_iota(jnp.int32, (SUB, width), 0) + hi * levels

    def flags(row, solid):
        for t in range(tiles):
            mask[row, t * SUB:(t + 1) * SUB, :] = jnp.where(level + t * SUB >= solid, 1.0, 0.0)

    for r in range(rows):
        flags(r, g_in[r:r + 1, :])
    ground_copy.wait_recv()
    for r in range(extra):
        flags(rows + r, ground[r:r + 1, :])

    def stage_row(row, k, step, slot, offset):
        nxt = 1 - slot
        stage = k % 4
        made = {}
        for t in range(tiles):
            level_at = slice(t * SUB, (t + 1) * SUB)
            for j in range(blocks):
                at = slice(j * LANES, (j + 1) * LANES)
                slopes = []
                for f in range(4):
                    c = cur[slot, f, row + 2, level_at, at]
                    d_r = 8.0 * (cur[slot, f, row + 3, level_at, at] - cur[slot, f, row + 1, level_at, at]) - (
                        cur[slot, f, row + 4, level_at, at] - cur[slot, f, row, level_at, at])
                    if j + 1 < blocks:
                        right = cur[slot, f, row + 2, level_at, (j + 1) * LANES:(j + 2) * LANES]
                    else:
                        right = small
                    if j:
                        left = cur[slot, f, row + 2, level_at, (j - 1) * LANES:j * LANES]
                    else:
                        left = small
                    p1 = pltpu.roll(jnp.where(lane < 1, right, c), LANES - 1, 1)
                    p2 = pltpu.roll(jnp.where(lane < 2, right, c), LANES - 2, 1)
                    m1 = pltpu.roll(jnp.where(lane >= LANES - 1, left, c), 1, 1)
                    m2 = pltpu.roll(jnp.where(lane >= LANES - 2, left, c), 2, 1)
                    d_c = 8.0 * (p1 - m1) - (p2 - m2)
                    if t + 1 < tiles:
                        top = cur[slot, f, row + 2, (t + 1) * SUB:(t + 2) * SUB, at]
                    else:
                        top = halo[slot, 1, f, row]
                        if j:
                            top = pltpu.roll(top, SUB - 2 * j, 0)
                    if t:
                        foot = cur[slot, f, row + 2, (t - 1) * SUB:t * SUB, at]
                    else:
                        foot = halo[slot, 0, f, row]
                        if (SUB - 2 - 2 * j) % SUB:
                            foot = pltpu.roll(foot, (SUB - 2 - 2 * j) % SUB, 0)
                    p1 = pltpu.roll(jnp.where(sub < 1, top, c), SUB - 1, 0)
                    p2 = pltpu.roll(jnp.where(sub < 2, top, c), SUB - 2, 0)
                    m1 = pltpu.roll(jnp.where(sub >= SUB - 1, foot, c), 1, 0)
                    m2 = pltpu.roll(jnp.where(sub >= SUB - 2, foot, c), 2, 0)
                    d_h = 8.0 * (p1 - m1) - (p2 - m2)
                    slopes.append((d_r, d_c, d_h))
                a_r = wind[0, row + offset, level_at, at] - 1.0
                a_c = wind[1, row + offset, level_at, at]
                a_h = wind[2, row + offset, level_at, at]
                fluid = mask[row + offset, level_at, at]
                p, u, v, w = slopes
                direct = [u[0] + v[1] + w[2], p[0], p[1], p[2]]
                for f in range(4):
                    d_r, d_c, d_h = slopes[f]
                    change = a_r * d_r + a_c * d_c + a_h * d_h + direct[f]
                    start = (a_ref if step == 0 else base)[f, row, level_at, at]
                    if stage == 0:
                        acc[f, row, level_at, at] = change
                    elif stage < 3:
                        acc[f, row, level_at, at] = acc[f, row, level_at, at] + 2.0 * change
                    if stage < 3:
                        new = (start - ((0.4 if stage == 2 else 0.2) / 12.0) * change) * fluid
                    else:
                        new = (start - (0.4 / 72.0) * (acc[f, row, level_at, at] + change)) * fluid
                    if k == 4 * steps - 1:
                        o_ref[f, row, level_at, at] = new
                        continue
                    if stage == 3:
                        base[f, row, level_at, at] = new
                    cur[nxt, f, row + 2, level_at, at] = new
                    made[f, t, j] = new
        if k < 4 * steps - 1:
            for f in range(4):
                pack_row(
                    nxt, f, row,
                    [made[f, 0, j] for j in range(blocks)], [made[f, tiles - 1, j] for j in range(blocks)])

    last = 4 * steps - 1
    offset = 0
    for k in range(4 * steps):
        step, slot = k // 4, k % 2
        nxt = 1 - slot
        if k % 4 == 0:
            offset = offset + shifts_ref[step]
        if k == 0:
            for later in range(steps):
                wind_copy(later).wait_recv()
        if k >= 1:
            drain(nxt)
        offset_now = offset

        def run(part, k=k, step=step, slot=slot, offset_now=offset_now):
            first, count = spans[part]

            def body(i, carry):
                stage_row(first + i, k, step, slot, offset_now)
                return carry

            lax.fori_loop(0, count, body, 0)

        recv_height(slot, 1)
        run(1)
        if k < last:
            send_height(nxt, 1)
        recv_height(slot, 0)
        pl.when(has_below)(lambda slot=slot: to_above(slot).wait_recv())
        run(0)
        if k < last:
            pl.when(has_below)(lambda nxt=nxt: to_below(nxt).start())
            send_height(nxt, 0)
        recv_height(slot, 2)
        pl.when(has_above)(lambda slot=slot: to_below(slot).wait_recv())
        run(2)
        if k < last:
            pl.when(has_above)(lambda nxt=nxt: to_above(nxt).start())
            send_height(nxt, 2)
    drain(last % 2)
    for step in range(steps):
        wind_copy(step).wait_send()
    ground_copy.wait_send()


def on_device(n_range, n_height, acoustic, mean_wind, ground, shifts):
    _, rows, levels, width = acoustic.shape
    steps = shifts.shape[0]
    vmem = pl.BlockSpec(memory_space=pltpu.VMEM)
    return pl.pallas_call(
        functools.partial(kernel, n_range, n_height, steps),
        out_shape=jax.ShapeDtypeStruct(acoustic.shape, jnp.float32),
        in_specs=[pl.BlockSpec(memory_space=pltpu.SMEM), vmem, vmem, vmem],
        out_specs=vmem,
        scratch_shapes=[
            pltpu.VMEM((2, 4, rows + 4, levels, width), jnp.float32),
            pltpu.VMEM(acoustic.shape, jnp.float32),
            pltpu.VMEM(acoustic.shape, jnp.float32),
            pltpu.VMEM((3, rows + SMAX * steps, levels, width), jnp.float32),
            pltpu.VMEM((rows + SMAX * steps, levels, width), jnp.float32),
            pltpu.VMEM((rows, width), jnp.int32),
            pltpu.VMEM((2, 2, 4, rows, SUB, LANES), jnp.float32),
            pltpu.VMEM((2, 2, 4, rows, SUB, LANES), jnp.float32),
            pltpu.SemaphoreType.DMA((2, 8)),
            pltpu.SemaphoreType.DMA((2, 8)),
            pltpu.SemaphoreType.DMA((steps + 1,)),
            pltpu.SemaphoreType.DMA((steps + 1,)),
        ],
        compiler_params=pltpu.CompilerParams(
            collective_id=0, has_side_effects=True, vmem_limit_bytes=40 * 1024 * 1024),
    )(shifts, acoustic, mean_wind, ground)


def solution(mesh):
    spec = P(None, "range", "height", None)
    return jax.shard_map(
        functools.partial(on_device, mesh.shape["range"], mesh.shape["height"]),
        mesh=mesh, in_specs=(spec, spec, P("range", None), P()), out_specs=spec, check_vma=False)
```

time: 172 us -> 46.9 us (0.27)
  the two profiles are of different devices: /device:TPU:26 before, /device:TPU:17 now
where the time goes in v1:
time: 46.9 us; the launch traced here: 46.7 us
  Pallas kernels  42.4 us (90%)
  local copies, waits for them, and re-layouts  4.2 us (9%)
    pallas_call x1, Pallas kernels, on_device(): pl.pallas_call(functools.partial(kernel, n_range, n_height, steps), out_s...  42.4 us
    unnamed x9, local copies, waits for them, and re-layouts  4.2 us

profile of v1, /device:TPU:17, one launch (start us, length us, event | category | flops | bytes accessed | tf_op | source)
XLA Modules:
  0.0 46.7 jit_solution(22909099460753808)
XLA Ops:
  0.0 0.0 copy-start
  0.0 1.0 %copy-done = f32[4,8,8,512]{3,2,1,0:T(8,128)S(1)} copy-done((f32[4,8,8,512]{3,2,1,0:T(8,128)S(1)}, f32[4,8,8,512]{3,2,1,0:T(8,128)}, u32[]{:S(2)}) %copy-start) | copy-done | bytes 524312
  1.0 0.0 copy-start.1
  1.0 1.0 %copy-done.1 = f32[3,8,8,512]{3,2,1,0:T(8,128)S(1)} copy-done((f32[3,8,8,512]{3,2,1,0:T(8,128)S(1)}, f32[3,8,8,512]{3,2,1,0:T(8,128)}, u32[]{:S(2)}) %copy-start.1) | copy-done | bytes 393240
  2.0 0.0 copy-start.2
  2.0 0.7 %copy-done.2 = s32[8,512]{1,0:T(8,128)S(1)} copy-done((s32[8,512]{1,0:T(8,128)S(1)}, s32[8,512]{1,0:T(8,128)}, u32[]{:S(2)}) %copy-start.2) | copy-done | bytes 16408
  2.8 0.0 copy-start.3
  2.8 0.7 %copy-done.3 = s32[2]{0:T(128)S(1)} copy-done((s32[2]{0:T(128)S(1)}, s32[2]{0:T(128)}, u32[]{:S(2)}) %copy-start.3) | copy-done | bytes 32
  3.4 42.4 %shard_map.46 = f32[4,8,8,512]{3,2,1,0:T(8,128)S(1)} custom-call(s32[2]{0:T(128)S(1)} %copy-done.3, f32[4,8,8,512]{3,2,1,0:T(8,128)S(1)} %copy-done, f32[3,8,8,512]{3,2,1,0:T(8,128)S(1)} %copy-done.1, s32[8,512]{1,0:T(8,128)S(1)} %copy-done.2), custom_call_target="tpu_custom_call" | custom-call | tf_op jit(solution)/shard_map/pallas_call | solution.py:317
  45.9 0.8 %copy.6 = f32[4,8,8,512]{3,2,1,0:T(8,128)} copy(f32[4,8,8,512]{3,2,1,0:T(8,128)S(1)} %shard_map.46) | data formatting | bytes 1048576
Async XLA Ops:
  0.0 1.0 %copy-start = (f32[4,8,8,512]{3,2,1,0:T(8,128)S(1)}, f32[4,8,8,512]{3,2,1,0:T(8,128)}, u32[]{:S(2)}) copy-start(f32[4,8,8,512]{3,2,1,0:T(8,128)} %a_ref.1) | copy-start | bytes 1572868
  1.0 1.0 %copy-start.1 = (f32[3,8,8,512]{3,2,1,0:T(8,128)S(1)}, f32[3,8,8,512]{3,2,1,0:T(8,128)}, u32[]{:S(2)}) copy-start(f32[3,8,8,512]{3,2,1,0:T(8,128)} %w_in.1) | copy-start | bytes 1179652
  2.0 0.7 %copy-start.2 = (s32[8,512]{1,0:T(8,128)S(1)}, s32[8,512]{1,0:T(8,128)}, u32[]{:S(2)}) copy-start(s32[8,512]{1,0:T(8,128)} %g_in.1) | copy-start | bytes 49156
  2.8 0.7 %copy-start.3 = (s32[2]{0:T(128)S(1)}, s32[2]{0:T(128)}, u32[]{:S(2)}) copy-start(s32[2]{0:T(128)} %shifts_ref.1) | copy-start | bytes 28

commit v2 on v1

--- a/solution.py
+++ b/solution.py
@@ -16,7 +16,7 @@
 def kernel(
     n_range, n_height, steps,
     shifts_ref, a_ref, w_in, g_in, o_ref,
-    cur, base, acc, wind, mask, ground, pack, halo, send_sem, recv_sem, wsend, wrecv,
+    cur, base, acc, own, top, wind, mask, solid, ground, pack, halo, send_sem, recv_sem, wsend, wrecv, local,
 ):
     rows, levels, width = a_ref.shape[1], a_ref.shape[2], a_ref.shape[3]
     tiles, blocks = levels // SUB, width // LANES
@@ -31,6 +31,14 @@
     sub = lax.broadcasted_iota(jnp.int32, (SUB, LANES), 0)
     lane = lax.broadcasted_iota(jnp.int32, (SUB, LANES), 1)
 
+    fetches = [
+        pltpu.make_async_copy(a_ref, cur.at[0, :, pl.ds(2, rows)], local.at[0]),
+        pltpu.make_async_copy(g_in, solid, local.at[1]),
+        pltpu.make_async_copy(a_ref, base, local.at[2]),
+        pltpu.make_async_copy(w_in, own, local.at[3]),
+        pltpu.make_async_copy(w_in.at[:, pl.ds(rows - 2, 2)], top.at[:, pl.ds(0, 2)], local.at[4]),
+        pltpu.make_async_copy(w_in, wind.at[:, pl.ds(0, rows)], local.at[5]),
+    ]
     barrier = pltpu.get_barrier_semaphore()
     pl.semaphore_signal(barrier, inc=1, device_id={"range": wrap_below}, device_id_type=MESH)
     pl.semaphore_signal(barrier, inc=1, device_id={"range": wrap_above}, device_id_type=MESH)
@@ -42,6 +50,9 @@
     @pl.when(has_up)
     def _():
         pl.semaphore_signal(barrier, inc=1, device_id={"height": hi + 1}, device_id_type=MESH)
+
+    for fetch in fetches:
+        fetch.start()
 
     def pack_row(slot, field, row, low, high):
         down, up = low[0], None
@@ -56,17 +67,6 @@
         pack[slot, 0, field, row] = down
         pack[slot, 1, field, row] = up
 
-    def load_row(row, carry):
-        for f in range(4):
-            for t in range(tiles):
-                cur[0, f, row + 2, t * SUB:(t + 1) * SUB, :] = a_ref[f, row, t * SUB:(t + 1) * SUB, :]
-            low = [a_ref[f, row, 0:SUB, j * LANES:(j + 1) * LANES] for j in range(blocks)]
-            high = [a_ref[f, row, levels - SUB:levels, j * LANES:(j + 1) * LANES] for j in range(blocks)]
-            pack_row(0, f, row, low, high)
-        return carry
-
-    lax.fori_loop(0, rows, load_row, 0)
-
     nothing = jnp.zeros((SUB, width), jnp.float32)
 
     @pl.when(jnp.logical_not(has_below))
@@ -101,6 +101,24 @@
                 for r in range(rows):
                     halo[s, 1, f, r] = small
 
+    level = lax.broadcasted_iota(jnp.int32, (SUB, width), 0) + hi * levels
+
+    def flags(row, foot):
+        for t in range(tiles):
+            mask[row, t * SUB:(t + 1) * SUB, :] = jnp.where(level + t * SUB >= foot, 1.0, 0.0)
+
+    def load_row(row, carry):
+        for f in range(4):
+            low = [cur[0, f, row + 2, 0:SUB, j * LANES:(j + 1) * LANES] for j in range(blocks)]
+            high = [cur[0, f, row + 2, levels - SUB:levels, j * LANES:(j + 1) * LANES] for j in range(blocks)]
+            pack_row(0, f, row, low, high)
+        return carry
+
+    fetches[0].wait()
+    lax.fori_loop(0, rows, load_row, 0)
+    fetches[1].wait()
+    for r in range(rows):
+        flags(r, solid[r:r + 1, :])
     pl.semaphore_wait(barrier, 2 + has_down.astype(jnp.int32) + has_up.astype(jnp.int32))
 
     def to_below(slot):
@@ -153,14 +171,16 @@
         pl.when(has_down)(down)
         pl.when(has_up)(up)
 
-    def wind_copy(step):
-        return pltpu.make_async_remote_copy(
-            src_ref=w_in.at[:, pl.ds(SMAX * step, SMAX)], dst_ref=wind.at[:, pl.ds(rows + SMAX * step, SMAX)],
-            send_sem=wsend.at[step], recv_sem=wrecv.at[step],
-            device_id={"range": wrap_below}, device_id_type=MESH)
-
+    wind_first = pltpu.make_async_remote_copy(
+        src_ref=w_in.at[:, pl.ds(0, SMAX)], dst_ref=top.at[:, pl.ds(2, SMAX)],
+        send_sem=wsend.at[0], recv_sem=wrecv.at[0],
+        device_id={"range": wrap_below}, device_id_type=MESH)
+    wind_rest = pltpu.make_async_remote_copy(
+        src_ref=w_in.at[:, pl.ds(SMAX, extra - SMAX)], dst_ref=wind.at[:, pl.ds(rows + SMAX, extra - SMAX)],
+        send_sem=wsend.at[1], recv_sem=wrecv.at[1],
+        device_id={"range": wrap_below}, device_id_type=MESH)
     ground_copy = pltpu.make_async_remote_copy(
-        src_ref=g_in, dst_ref=ground, send_sem=wsend.at[steps], recv_sem=wrecv.at[steps],
+        src_ref=g_in, dst_ref=ground, send_sem=wsend.at[2], recv_sem=wrecv.at[2],
         device_id={"range": wrap_below}, device_id_type=MESH)
 
     pl.when(has_below)(lambda: to_below(0).start())
@@ -168,29 +188,11 @@
     for part in (1, 0, 2):
         send_height(0, part)
     ground_copy.start()
-    for step in range(steps):
-        wind_copy(step).start()
-
-    def own_wind(row, carry):
-        for c in range(3):
-            for t in range(tiles):
-                wind[c, row, t * SUB:(t + 1) * SUB, :] = w_in[c, row, t * SUB:(t + 1) * SUB, :]
-        return carry
-
-    lax.fori_loop(0, rows, own_wind, 0)
-    level = lax.broadcasted_iota(jnp.int32, (SUB, width), 0) + hi * levels
-
-    def flags(row, solid):
-        for t in range(tiles):
-            mask[row, t * SUB:(t + 1) * SUB, :] = jnp.where(level + t * SUB >= solid, 1.0, 0.0)
-
-    for r in range(rows):
-        flags(r, g_in[r:r + 1, :])
-    ground_copy.wait_recv()
-    for r in range(extra):
-        flags(rows + r, ground[r:r + 1, :])
-
-    def stage_row(row, k, step, slot, offset):
+    wind_first.start()
+    fetches[2].wait()
+    fetches[3].wait()
+
+    def stage_row(row, k, step, slot, offset, air, air_row):
         nxt = 1 - slot
         stage = k % 4
         made = {}
@@ -234,16 +236,16 @@
                     m2 = pltpu.roll(jnp.where(sub >= SUB - 2, foot, c), 2, 0)
                     d_h = 8.0 * (p1 - m1) - (p2 - m2)
                     slopes.append((d_r, d_c, d_h))
-                a_r = wind[0, row + offset, level_at, at] - 1.0
-                a_c = wind[1, row + offset, level_at, at]
-                a_h = wind[2, row + offset, level_at, at]
+                a_r = air[0, air_row, level_at, at] - 1.0
+                a_c = air[1, air_row, level_at, at]
+                a_h = air[2, air_row, level_at, at]
                 fluid = mask[row + offset, level_at, at]
                 p, u, v, w = slopes
                 direct = [u[0] + v[1] + w[2], p[0], p[1], p[2]]
                 for f in range(4):
                     d_r, d_c, d_h = slopes[f]
                     change = a_r * d_r + a_c * d_c + a_h * d_h + direct[f]
-                    start = (a_ref if step == 0 else base)[f, row, level_at, at]
+                    start = base[f, row, level_at, at]
                     if stage == 0:
                         acc[f, row, level_at, at] = change
                     elif stage < 3:
@@ -252,10 +254,7 @@
                         new = (start - ((0.4 if stage == 2 else 0.2) / 12.0) * change) * fluid
                     else:
                         new = (start - (0.4 / 72.0) * (acc[f, row, level_at, at] + change)) * fluid
-                    if k == 4 * steps - 1:
-                        o_ref[f, row, level_at, at] = new
-                        continue
-                    if stage == 3:
+                    if stage == 3 and k < 4 * steps - 1:
                         base[f, row, level_at, at] = new
                     cur[nxt, f, row + 2, level_at, at] = new
                     made[f, t, j] = new
@@ -266,15 +265,24 @@
                     [made[f, 0, j] for j in range(blocks)], [made[f, tiles - 1, j] for j in range(blocks)])
 
     last = 4 * steps - 1
+    results = [
+        pltpu.make_async_copy(
+            cur.at[1 - last % 2, :, pl.ds(2 + first, count)], o_ref.at[:, pl.ds(first, count)], local.at[6 + part])
+        for part, (first, count) in enumerate(spans)
+    ]
     offset = 0
     for k in range(4 * steps):
         step, slot = k // 4, k % 2
         nxt = 1 - slot
         if k % 4 == 0:
             offset = offset + shifts_ref[step]
-        if k == 0:
-            for later in range(steps):
-                wind_copy(later).wait_recv()
+        if k == 4:
+            fetches[5].wait()
+            wind_rest.wait_recv()
+            for c in range(3):
+                for r in range(SMAX):
+                    for t in range(tiles):
+                        wind[c, rows + r, t * SUB:(t + 1) * SUB, :] = top[c, 2 + r, t * SUB:(t + 1) * SUB, :]
         if k >= 1:
             drain(nxt)
         offset_now = offset
@@ -283,7 +291,13 @@
             first, count = spans[part]
 
             def body(i, carry):
-                stage_row(first + i, k, step, slot, offset_now)
+                row = first + i
+                if step:
+                    stage_row(row, k, step, slot, offset_now, wind, row + offset_now)
+                elif part < 2:
+                    stage_row(row, k, step, slot, offset_now, own, row + offset_now)
+                else:
+                    stage_row(row, k, step, slot, offset_now, top, row + offset_now - (rows - 2))
                 return carry
 
             lax.fori_loop(0, count, body, 0)
@@ -292,49 +306,68 @@
         run(1)
         if k < last:
             send_height(nxt, 1)
+        else:
+            results[1].start()
+        if k == 1:
+            wind_rest.start()
         recv_height(slot, 0)
         pl.when(has_below)(lambda slot=slot: to_above(slot).wait_recv())
         run(0)
         if k < last:
             pl.when(has_below)(lambda nxt=nxt: to_below(nxt).start())
             send_height(nxt, 0)
+        else:
+            results[0].start()
         recv_height(slot, 2)
         pl.when(has_above)(lambda slot=slot: to_below(slot).wait_recv())
+        if k == 0:
+            fetches[4].wait()
+            wind_first.wait_recv()
+            ground_copy.wait_recv()
+            for r in range(extra):
+                flags(rows + r, ground[r:r + 1, :])
         run(2)
         if k < last:
             pl.when(has_above)(lambda nxt=nxt: to_above(nxt).start())
             send_height(nxt, 2)
+        else:
+            results[2].start()
     drain(last % 2)
-    for step in range(steps):
-        wind_copy(step).wait_send()
-    ground_copy.wait_send()
+    for copy in (wind_first, wind_rest, ground_copy):
+        copy.wait_send()
+    for result in results:
+        result.wait()
 
 
 def on_device(n_range, n_height, acoustic, mean_wind, ground, shifts):
     _, rows, levels, width = acoustic.shape
     steps = shifts.shape[0]
-    vmem = pl.BlockSpec(memory_space=pltpu.VMEM)
+    hbm = pl.BlockSpec(memory_space=pltpu.HBM)
     return pl.pallas_call(
         functools.partial(kernel, n_range, n_height, steps),
         out_shape=jax.ShapeDtypeStruct(acoustic.shape, jnp.float32),
-        in_specs=[pl.BlockSpec(memory_space=pltpu.SMEM), vmem, vmem, vmem],
-        out_specs=vmem,
+        in_specs=[pl.BlockSpec(memory_space=pltpu.SMEM), hbm, hbm, hbm],
+        out_specs=hbm,
         scratch_shapes=[
             pltpu.VMEM((2, 4, rows + 4, levels, width), jnp.float32),
             pltpu.VMEM(acoustic.shape, jnp.float32),
             pltpu.VMEM(acoustic.shape, jnp.float32),
+            pltpu.VMEM((3, rows, levels, width), jnp.float32),
+            pltpu.VMEM((3, 2 + SMAX, levels, width), jnp.float32),
             pltpu.VMEM((3, rows + SMAX * steps, levels, width), jnp.float32),
             pltpu.VMEM((rows + SMAX * steps, levels, width), jnp.float32),
+            pltpu.VMEM((rows, width), jnp.int32),
             pltpu.VMEM((rows, width), jnp.int32),
             pltpu.VMEM((2, 2, 4, rows, SUB, LANES), jnp.float32),
             pltpu.VMEM((2, 2, 4, rows, SUB, LANES), jnp.float32),
             pltpu.SemaphoreType.DMA((2, 8)),
             pltpu.SemaphoreType.DMA((2, 8)),
-            pltpu.SemaphoreType.DMA((steps + 1,)),
-            pltpu.SemaphoreType.DMA((steps + 1,)),
+            pltpu.SemaphoreType.DMA((3,)),
+            pltpu.SemaphoreType.DMA((3,)),
+            pltpu.SemaphoreType.DMA((9,)),
         ],
         compiler_params=pltpu.CompilerParams(
-            collective_id=0, has_side_effects=True, vmem_limit_bytes=40 * 1024 * 1024),
+            collective_id=0, has_side_effects=True, vmem_limit_bytes=64 * 1024 * 1024 - 65536),
     )(shifts, acoustic, mean_wind, ground)
 
 

time: 46.9 us -> 44.1 us (0.940)
  the two profiles are of different devices: /device:TPU:17 before, /device:TPU:1 now
where the time goes in v2:
time: 44.1 us; the launch traced here: 44 us
  Pallas kernels  42.1 us (95%)
  local copies, waits for them, and re-layouts  1.87 us (4%)
    pallas_call x1, Pallas kernels, on_device(): pl.pallas_call(functools.partial(kernel, n_range, n_height, steps), out_s...  42.1 us
    unnamed x1, local copies, waits for them, and re-layouts  1.87 us

profile of v2, /device:TPU:1, one launch (start us, length us, event | category | flops | bytes accessed | tf_op | source)
XLA Modules:
  0.0 44.0 jit_solution(9500113516013618650)
XLA Ops:
  0.0 42.1 %shard_map.46 = f32[4,8,8,512]{3,2,1,0:T(8,128)} custom-call(s32[2]{0:T(128)} %shifts_ref.1, f32[4,8,8,512]{3,2,1,0:T(8,128)} %a_ref.1, f32[3,8,8,512]{3,2,1,0:T(8,128)} %w_in.1, s32[8,512]{1,0:T(8,128)} %g_in.1), custom_call_target="tpu_custom_call" | custom-call | tf_op jit(solution)/shard_map/pallas_call | solution.py:346
  42.1 1.9 %copy.6 = f32[4,8,8,512]{3,2,1,0:T(8,128)} copy(f32[4,8,8,512]{3,2,1,0:T(8,128)} %shard_map.46) | data formatting | bytes 1048576

commit v3 on v2

--- a/solution.py
+++ b/solution.py
@@ -121,16 +121,16 @@
         flags(r, solid[r:r + 1, :])
     pl.semaphore_wait(barrier, 2 + has_down.astype(jnp.int32) + has_up.astype(jnp.int32))
 
-    def to_below(slot):
+    def to_below(slot, i):
         return pltpu.make_async_remote_copy(
-            src_ref=cur.at[slot, :, pl.ds(2, 2)], dst_ref=cur.at[slot, :, pl.ds(rows + 2, 2)],
-            send_sem=send_sem.at[slot, 0], recv_sem=recv_sem.at[slot, 0],
+            src_ref=cur.at[slot, :, pl.ds(2 + i, 1)], dst_ref=cur.at[slot, :, pl.ds(rows + 2 + i, 1)],
+            send_sem=send_sem.at[slot, 8 + i], recv_sem=recv_sem.at[slot, 8 + i],
             device_id={"range": below}, device_id_type=MESH)
 
-    def to_above(slot):
+    def to_above(slot, i):
         return pltpu.make_async_remote_copy(
-            src_ref=cur.at[slot, :, pl.ds(rows, 2)], dst_ref=cur.at[slot, :, pl.ds(0, 2)],
-            send_sem=send_sem.at[slot, 1], recv_sem=recv_sem.at[slot, 1],
+            src_ref=cur.at[slot, :, pl.ds(rows + i, 1)], dst_ref=cur.at[slot, :, pl.ds(i, 1)],
+            send_sem=send_sem.at[slot, i], recv_sem=recv_sem.at[slot, i],
             device_id={"range": above}, device_id_type=MESH)
 
     spans = [(0, 2), (2, rows - 4), (rows - 2, 2)]
@@ -166,8 +166,9 @@
             for part in range(3):
                 to_up(slot, part).wait_send()
 
-        pl.when(has_below)(lambda: to_below(slot).wait_send())
-        pl.when(has_above)(lambda: to_above(slot).wait_send())
+        for i in range(2):
+            pl.when(has_below)(lambda i=i: to_below(slot, i).wait_send())
+            pl.when(has_above)(lambda i=i: to_above(slot, i).wait_send())
         pl.when(has_down)(down)
         pl.when(has_up)(up)
 
@@ -183,8 +184,9 @@
         src_ref=g_in, dst_ref=ground, send_sem=wsend.at[2], recv_sem=wrecv.at[2],
         device_id={"range": wrap_below}, device_id_type=MESH)
 
-    pl.when(has_below)(lambda: to_below(0).start())
-    pl.when(has_above)(lambda: to_above(0).start())
+    for i in range(2):
+        pl.when(has_below)(lambda i=i: to_below(0, i).start())
+        pl.when(has_above)(lambda i=i: to_above(0, i).start())
     for part in (1, 0, 2):
         send_height(0, part)
     ground_copy.start()
@@ -287,8 +289,10 @@
             drain(nxt)
         offset_now = offset
 
-        def run(part, k=k, step=step, slot=slot, offset_now=offset_now):
+        def run(part, chosen=None, k=k, step=step, slot=slot, offset_now=offset_now):
             first, count = spans[part]
+            if chosen is not None:
+                first, count = first + chosen, 1
 
             def body(i, carry):
                 row = first + i
@@ -311,24 +315,30 @@
         if k == 1:
             wind_rest.start()
         recv_height(slot, 0)
-        pl.when(has_below)(lambda slot=slot: to_above(slot).wait_recv())
-        run(0)
+        for i in range(2):
+            pl.when(has_below)(lambda slot=slot, i=i: to_above(slot, i).wait_recv())
+        for i in range(2):
+            run(0, i)
+            if k < last:
+                pl.when(has_below)(lambda nxt=nxt, i=i: to_below(nxt, i).start())
         if k < last:
-            pl.when(has_below)(lambda nxt=nxt: to_below(nxt).start())
             send_height(nxt, 0)
         else:
             results[0].start()
         recv_height(slot, 2)
-        pl.when(has_above)(lambda slot=slot: to_below(slot).wait_recv())
+        for i in range(2):
+            pl.when(has_above)(lambda slot=slot, i=i: to_below(slot, i).wait_recv())
         if k == 0:
             fetches[4].wait()
             wind_first.wait_recv()
             ground_copy.wait_recv()
             for r in range(extra):
                 flags(rows + r, ground[r:r + 1, :])
-        run(2)
+        for i in range(2):
+            run(2, i)
+            if k < last:
+                pl.when(has_above)(lambda nxt=nxt, i=i: to_above(nxt, i).start())
         if k < last:
-            pl.when(has_above)(lambda nxt=nxt: to_above(nxt).start())
             send_height(nxt, 2)
         else:
             results[2].start()
@@ -360,8 +370,8 @@
             pltpu.VMEM((rows, width), jnp.int32),
             pltpu.VMEM((2, 2, 4, rows, SUB, LANES), jnp.float32),
             pltpu.VMEM((2, 2, 4, rows, SUB, LANES), jnp.float32),
-            pltpu.SemaphoreType.DMA((2, 8)),
-            pltpu.SemaphoreType.DMA((2, 8)),
+            pltpu.SemaphoreType.DMA((2, 10)),
+            pltpu.SemaphoreType.DMA((2, 10)),
             pltpu.SemaphoreType.DMA((3,)),
             pltpu.SemaphoreType.DMA((3,)),
             pltpu.SemaphoreType.DMA((9,)),

time: 44.1 us -> 43.9 us (level); the launches traced: 44 us -> 43.3 us
  Pallas kernels: 42.1 us -> 41.4 us
    pallas_call x1, Pallas kernels: 42.1 us -> 41.4 us  [on_device(): pl.pallas_call(functools.partial(kernel, n_range, n_height, steps), out_s...]
where the time goes in v3:
time: 43.9 us; the launch traced here: 43.3 us
  Pallas kernels  41.4 us (94%)
  local copies, waits for them, and re-layouts  1.87 us (4%)
    pallas_call x1, Pallas kernels, on_device(): pl.pallas_call(functools.partial(kernel, n_range, n_height, steps), out_s...  41.4 us
    unnamed x1, local copies, waits for them, and re-layouts  1.87 us

profile of v3, /device:TPU:1, one launch (start us, length us, event | category | flops | bytes accessed | tf_op | source)
XLA Modules:
  0.0 43.3 jit_solution(8135073772540660940)
XLA Ops:
  0.0 41.4 %shard_map.46 = f32[4,8,8,512]{3,2,1,0:T(8,128)} custom-call(s32[2]{0:T(128)} %shifts_ref.1, f32[4,8,8,512]{3,2,1,0:T(8,128)} %a_ref.1, f32[3,8,8,512]{3,2,1,0:T(8,128)} %w_in.1, s32[8,512]{1,0:T(8,128)} %g_in.1), custom_call_target="tpu_custom_call" | custom-call | tf_op jit(solution)/shard_map/pallas_call | solution.py:356
  41.4 1.9 %copy.6 = f32[4,8,8,512]{3,2,1,0:T(8,128)} copy(f32[4,8,8,512]{3,2,1,0:T(8,128)} %shard_map.46) | data formatting | bytes 1048576
